TPU v7x, 32 devices: a whole 2x2x4 slice. The times are simulated.
32 devices in a mesh: wide: 8 (over y, x, core), narrow: 4 (over z).
Axes of the slice: x: 2, y: 2, z: 4, core: 2. Of those that a mesh axis runs over, the one named last changes fastest.
Arguments:
- blocks: bfloat16 [8, 4, 16, 64, 4096], P('wide', 'narrow'), may hold values from -16 to 16
- row_tile: int32 [8, 4, 16], P('wide', 'narrow'), may hold values from 0 to 7
- col_tile: int32 [8, 4, 16], P('wide', 'narrow'), may hold values from 0 to 15, as said below
- depth_tile: int32 [8, 4, 16], P('wide', 'narrow'), may hold values from 0 to 15
- block_count: int32 [8, 4], P('wide', 'narrow'), may hold values from 4 to 16, as said below
- factor_b: bfloat16 [4096, 256], P(('wide', 'narrow')), may hold values from -40 to 40
- factor_c: bfloat16 [1024, 256], replicated, may hold values from -0.61035156 to 0.61035156
Outputs:
- a_new: float32 [4096, 256], P(('wide', 'narrow'))
- b_new: float32 [4096, 256], P(('wide', 'narrow'))
Inputs may be any that keep to these rules, and one draw needn't show every extreme that they name: `block_count`: every device holds at least 4 live blocks, and some device exactly 16. col_tile // 2 is the index of wide that holds the block's mode-2 factor rows; among the 16 slots of one device, live or not, each such index appears at most 2 times, and some index exactly 2 times.
All inputs are finite; a program needn't handle non-finite values.
Results may differ from a plain program's by a relative error of at most 0.02.
Values may be sent and summed in bfloat16 or wider, within the bound.
A program may use at most 128 MiB of HBM per device.

v0:
```python
import functools

import jax
import jax.numpy as jnp
from jax import lax
from jax.experimental import pallas as pl
from jax.experimental.pallas import tpu as pltpu
from jax.sharding import PartitionSpec as P

VMEM = pl.BlockSpec(memory_space=pltpu.VMEM)
HIGH = lax.Precision.HIGHEST
NB = 64


def dot(x, y, x_dim, y_dim, precision=None):
    return lax.dot_general(
        x, y, (((x_dim,), (y_dim,)), ((), ())), precision=precision,
        preferred_element_type=jnp.float32,
    )


def pass_kernel(first, rows, load_id, store_id, depth_id, count, x_ref, c_ref, f_ref, out_ref):
    slot = pl.program_id(0)

    @pl.when(slot == 0)
    def _():
        out_ref[...] = jnp.zeros_like(out_ref)

    @pl.when(slot < count[0])
    def _():
        depth_rows = c_ref[pl.ds(pl.multiple_of(depth_id[slot] * rows, rows), rows), :]
        tile = f_ref[pl.ds(pl.multiple_of(load_id[slot] * rows, rows), rows), :].astype(jnp.float32)
        target = pl.multiple_of(store_id[slot] * rows, rows)
        step = 8
        total = None
        for a in range(0, rows, step):
            x = x_ref[0, :, a * rows : (a + step) * rows]
            mix = dot(x, depth_rows, 0, 0).reshape(step, rows, -1)
            if first:
                at = pl.ds(target + a, step)
                out_ref[at, :] += jnp.sum(mix * tile[None], axis=1)
            else:
                term = jnp.sum(mix * tile[a : a + step][:, None, :], axis=0)
                total = term if total is None else total + term
        if not first:
            out_ref[pl.ds(target, rows), :] += total


def mix_pass(first, x, load_id, store_id, depth_id, count, c, f, out_rows):
    cap, rows, width = x.shape
    rank = c.shape[1]
    whole = lambda a: pl.BlockSpec(a.shape, lambda s, *_: (0, 0))
    return pl.pallas_call(
        functools.partial(pass_kernel, first, rows),
        out_shape=jax.ShapeDtypeStruct((out_rows, rank), jnp.float32),
        grid_spec=pltpu.PrefetchScalarGridSpec(
            num_scalar_prefetch=4,
            grid=(cap,),
            in_specs=[
                pl.BlockSpec(
                    (1, rows, width),
                    lambda s, l, t, d, n: (jnp.minimum(s, n[0] - 1), 0, 0),
                ),
                whole(c),
                whole(f),
            ],
            out_specs=pl.BlockSpec((out_rows, rank), lambda s, *_: (0, 0)),
        ),
        cost_estimate=pl.CostEstimate(
            flops=cap * rows * width * rank * 8, bytes_accessed=x.size * 2, transcendentals=0
        ),
        compiler_params=pltpu.CompilerParams(vmem_limit_bytes=40 * 1024 * 1024),
    )(load_id, store_id, depth_id, count, x, c, f)


def root_kernel(gram_ref, c_ref, w_ref, work):
    rank = gram_ref.shape[0]
    c = c_ref[...]
    work[:, :rank] = gram_ref[...] * dot(c, c, 0, 0)
    row_id = lax.broadcasted_iota(jnp.int32, (rank, rank), 0)
    col_id = lax.broadcasted_iota(jnp.int32, (rank, rank), 1)
    work[:, rank:] = (row_id == col_id).astype(jnp.float32)
    row = lax.broadcasted_iota(jnp.int32, (NB, 2 * NB), 0)
    lane = lax.broadcasted_iota(jnp.int32, (NB, 2 * NB), 1)
    wide_lane = lax.broadcasted_iota(jnp.int32, (NB, rank), 1)

    def block_step(k, carry):
        at = pl.ds(pl.multiple_of(k * NB, NB), NB)
        tile = work[at, pl.ds(pl.multiple_of(k // 2 * 2 * NB, 2 * NB), 2 * NB)]
        tile = jnp.where(k % 2 == 1, pltpu.roll(tile, NB, 1), tile)
        parts = jnp.where(lane < NB, tile, (lane - NB == row).astype(jnp.float32))
        parts = [parts[i : i + 8] for i in range(0, NB, 8)]
        sub = row[:8]
        for j in range(NB):
            top = j // 8
            cols = [jnp.broadcast_to(parts[i][:, j : j + 1], (8, 2 * NB)) for i in range(top, NB // 8)]
            pivot_row = parts[top][j % 8 : j % 8 + 1, :]
            scaled = pivot_row / cols[0][j % 8 : j % 8 + 1, :]
            for i in range(top, NB // 8):
                factor = cols[i - top]
                if i == top:
                    factor = jnp.where(sub > j % 8, factor, 0.0)
                parts[i] = parts[i] - factor * scaled
        done = jnp.concatenate(parts, axis=0)
        diag = jnp.sum(jnp.where(lane == row, done, 0.0), axis=1, keepdims=True)
        root = done * lax.rsqrt(diag)
        head = dot(root[:, NB:], work[at, :], 1, 0, HIGH)
        w_ref[at, :] = head[:, rank:]
        below = jnp.where(wide_lane >= (k + 1) * NB, head[:, :rank], 0.0)
        work[...] = work[...] - dot(below, head, 0, 0, HIGH)
        return carry

    lax.fori_loop(0, rank // NB, block_step, 0)


def inverse_root(gram, c):
    rank = gram.shape[0]
    return pl.pallas_call(
        root_kernel,
        out_shape=jax.ShapeDtypeStruct((rank, rank), jnp.float32),
        in_specs=[VMEM] * 2,
        out_specs=VMEM,
        scratch_shapes=[pltpu.VMEM((rank, 2 * rank), jnp.float32)],
        cost_estimate=pl.CostEstimate(flops=10**9, bytes_accessed=10**6, transcendentals=0),
        compiler_params=pltpu.CompilerParams(vmem_limit_bytes=40 * 1024 * 1024),
    )(gram, c)


def apply_kernel(m_ref, w_ref, new_ref, *rest):
    w = w_ref[...]
    new = dot(dot(m_ref[...], w, 1, 1, HIGH), w, 1, 0, HIGH)
    new_ref[...] = new
    if rest:
        half = new.astype(jnp.bfloat16)
        rest[0][...] = half
        rest[1][...] = dot(half, half, 0, 0)


def apply_root(m, w, more):
    rank = w.shape[0]
    out_shape = [jax.ShapeDtypeStruct(m.shape, jnp.float32)]
    if more:
        out_shape += [
            jax.ShapeDtypeStruct(m.shape, jnp.bfloat16),
            jax.ShapeDtypeStruct((rank, rank), jnp.float32),
        ]
    return pl.pallas_call(
        apply_kernel,
        out_shape=out_shape,
        in_specs=[VMEM] * 2,
        out_specs=[VMEM] * len(out_shape),
        compiler_params=pltpu.CompilerParams(vmem_limit_bytes=40 * 1024 * 1024),
    )(m, w)


def local(blocks, row_tile, col_tile, depth_tile, block_count, factor_b, factor_c):
    x = blocks[0, 0]
    first_ids = row_tile[0, 0]
    second_ids = col_tile[0, 0]
    depth_ids = depth_tile[0, 0]
    count = block_count[0]
    rows = x.shape[1]
    wide_count = lax.axis_size("wide")
    narrow_count = lax.axis_size("narrow")
    local_rows = factor_b.shape[0]

    gathered = lax.all_gather(factor_b, "wide", axis=0, tiled=True)
    gram_b = lax.psum(dot(factor_b, factor_b, 0, 0), ("wide", "narrow"))
    first_part = mix_pass(
        True, x, second_ids, first_ids, depth_ids, count, factor_c, gathered, narrow_count * local_rows
    )
    mttkrp_a = lax.psum_scatter(first_part, "narrow", scatter_dimension=0, tiled=True)
    root_a = inverse_root(gram_b, factor_c)
    a_new, a_half, gram_a = apply_root(mttkrp_a, root_a, True)
    a_rows = lax.all_gather(a_half, "narrow", axis=0, tiled=True)
    gram_a = lax.psum(gram_a, ("wide", "narrow"))
    second_part = mix_pass(
        False, x, first_ids, second_ids, depth_ids, count, factor_c, a_rows, wide_count * local_rows
    )
    mttkrp_b = lax.psum_scatter(second_part, "wide", scatter_dimension=0, tiled=True)
    root_b = inverse_root(gram_a, factor_c)
    (b_new,) = apply_root(mttkrp_b, root_b, False)
    return (a_new, b_new)


def solution(mesh):
    return jax.shard_map(
        local,
        mesh=mesh,
        in_specs=(
            P("wide", "narrow", None, None, None),
            P("wide", "narrow", None),
            P("wide", "narrow", None),
            P("wide", "narrow", None),
            P("wide", "narrow"),
            P(("wide", "narrow"), None),
            P(),
        ),
        out_specs=(P(("wide", "narrow"), None), P(("wide", "narrow"), None)),
        check_vma=False,
    )
```

profile of v0, /device:TPU:0, one launch (start us, length us, event | category | flops | bytes accessed | tf_op | source)
XLA Modules:
  0.0 345.9 jit_solution(13635811071580813545)
XLA Ops:
  8.0 1.8 fusion
  9.9 0.0 reduce-scatter.3.cloned.1.call-start
  10.0 11.6 %all_gather.6.f_ref = bf16[1024,256]{1,0:T(8,128)(2,1)S(1)} all-gather(bf16[128,256]{1,0:T(8,128)(2,1)} %param.12), channel_id=1, replica_groups=mesh['wide'=8,'narrow'=4] {'wide'}, dimensions={0}, use_global_device_ids=true | all-gather | bytes 589824 | tf_op jit(solution)/shard_map/all_gather | solution.py:167
  22.2 3.4 copy-done.2
  25.6 1.0 copy-done.4
  26.7 0.7 copy-done.8
  27.3 0.7 copy-done.10
  28.0 0.7 copy-done.12
  28.6 10.0 %shard_map.86 = f32[512,256]{1,0:T(8,128)} custom-call(s32[16]{0:T(128)S(1)} %bitcast.11, s32[16]{0:T(128)S(1)} %bitcast.13, s32[16]{0:T(128)S(1)} %bitcast.15, s32[1]{0:T(128)} %bitcast.7.count, bf16[16,64,4096]{2,1,0:T(8,128)(2,1)S(1)} %bitcast.9, bf16[1024,256]{1,0:T(8,128)(2,1)S(1)} %copy-done.4, bf16[1024,256]{1,0:T(8,128)(2,1)S(1)} %all_gather.6.f_ref), custom_call_target="tpu_custom_call" | custom-call | flops 8589934592 | bytes 8388608 | tf_op jit(solution)/shard_map/pallas_call | solution.py:53
  38.7 105.4 %all-reduce.3.cloned.1.call-done.gram_ref = f32[256,256]{1,0:T(8,128)} async-done(((f32[256,256]{1,0:T(8,128)}), f32[256,256]{1,0:T(8,128)}) %all-reduce.3.cloned.1.call-update) | async-done | bytes 262160 | tf_op jit(solution)/shard_map/psum | solution.py:168
  144.1 0.9 copy-done.6
  145.1 25.8 %shard_map.87.w_ref = f32[256,256]{1,0:T(8,128)S(1)} custom-call(f32[256,256]{1,0:T(8,128)S(1)} %copy-done.6, bf16[1024,256]{1,0:T(8,128)(2,1)S(1)} %copy-done.5), custom_call_target="tpu_custom_call" | custom-call | flops 1000000000 | bytes 1000000 | tf_op jit(solution)/shard_map/pallas_call | solution.py:118
  171.0 0.9 copy-done
  171.9 1.7 shard_map.88
  173.6 0.0 reduce-scatter.5.cloned.1.call-start
  173.6 14.4 %all_gather.7.f_ref = bf16[512,256]{1,0:T(8,128)(2,1)S(1)} all-gather(bf16[128,256]{1,0:T(8,128)(2,1)S(1)} %get-tuple-element.6), channel_id=1, replica_groups=mesh['wide'=8,'narrow'=4] {'narrow'}, dimensions={0}, use_global_device_ids=true | all-gather | bytes 327680 | tf_op jit(solution)/shard_map/all_gather | solution.py:175
  188.1 3.4 copy-done.3
  191.5 10.2 %shard_map.89 = f32[1024,256]{1,0:T(8,128)} custom-call(s32[16]{0:T(128)S(1)} %bitcast.14, s32[16]{0:T(128)S(1)} %bitcast.12, s32[16]{0:T(128)S(1)} %bitcast.16, s32[1]{0:T(128)} %bitcast.8.count, bf16[16,64,4096]{2,1,0:T(8,128)(2,1)S(1)} %bitcast.10, bf16[1024,256]{1,0:T(8,128)(2,1)S(1)} %copy-done.5, bf16[512,256]{1,0:T(8,128)(2,1)S(1)} %all_gather.7.f_ref), custom_call_target="tpu_custom_call" | custom-call | flops 8589934592 | bytes 8388608 | tf_op jit(solution)/shard_map/pallas_call | solution.py:53
  201.7 96.1 %all-reduce.5.cloned.1.call-done.gram_ref = f32[256,256]{1,0:T(8,128)} async-done(((f32[256,256]{1,0:T(8,128)}), f32[256,256]{1,0:T(8,128)}) %all-reduce.5.cloned.1.call-update) | async-done | bytes 262160 | tf_op jit(solution)/shard_map/psum | solution.py:176
  297.8 0.9 copy-done.7
  298.8 25.8 %shard_map.90.w_ref = f32[256,256]{1,0:T(8,128)S(1)} custom-call(f32[256,256]{1,0:T(8,128)S(1)} %copy-done.7, bf16[1024,256]{1,0:T(8,128)(2,1)S(1)} %copy-done.5), custom_call_target="tpu_custom_call" | custom-call | flops 1000000000 | bytes 1000000 | tf_op jit(solution)/shard_map/pallas_call | solution.py:118
  324.6 11.8 %reduce-scatter.5.cloned.1.call-done.m_ref = f32[128,256]{1,0:T(8,128)} async-done(((f32[1024,256]{1,0:T(8,128)}), f32[128,256]{1,0:T(8,128)}) %reduce-scatter.5.cloned.1.call-update) | async-done | bytes 131088 | tf_op jit(solution)/shard_map/reduce_scatter | solution.py:180
  336.4 0.9 copy-done.1
  337.3 1.4 shard_map.91
  (25 shorter events, 0.2 us)
Async XLA Ops:
  8.0 136.1 %all-reduce.3.cloned.1.call-start = ((), (), s32[]{:S(2)}) async-start(), calls=%async_computation.3 | async-start | bytes 524288 | tf_op jit(solution)/shard_map/psum | solution.py:168
  9.9 161.0 %reduce-scatter.3.cloned.1.call-start = ((), (), s32[]{:S(2)}) async-start(), calls=%async_computation.2 | async-start | bytes 655360 | tf_op jit(solution)/shard_map/reduce_scatter | solution.py:172
  22.2 3.4 copy-start.2
  25.6 1.0 copy-start.4
  26.7 0.7 copy-start.8
  27.3 0.7 copy-start.10
  28.0 0.7 copy-start.12
  28.6 115.5 %copy-start.5 = (bf16[1024,256]{1,0:T(8,128)(2,1)S(1)}, bf16[1024,256]{1,0:T(8,128)(2,1)}, u32[]{:S(2)}) copy-start(bf16[1024,256]{1,0:T(8,128)(2,1)} %c_ref.7) | copy-start | bytes 1572868
  28.6 159.4 %copy-start.9 = (s32[1,1,16]{2,1,0:T(1,128)S(1)}, s32[1,1,16]{2,1,0:T(1,128)}, u32[]{:S(2)}) copy-start(s32[1,1,16]{2,1,0:T(1,128)} %param.9) | copy-start | bytes 196
  28.6 159.4 %copy-start.11 = (s32[1,1,16]{2,1,0:T(1,128)S(1)}, s32[1,1,16]{2,1,0:T(1,128)}, u32[]{:S(2)}) copy-start(s32[1,1,16]{2,1,0:T(1,128)} %param.8) | copy-start | bytes 196
  28.6 159.4 %copy-start.13 = (s32[1,1,16]{2,1,0:T(1,128)S(1)}, s32[1,1,16]{2,1,0:T(1,128)}, u32[]{:S(2)}) copy-start(s32[1,1,16]{2,1,0:T(1,128)} %param.10) | copy-start | bytes 196
  38.7 259.1 %all-reduce.5.cloned.1.call-start = ((), (), s32[]{:S(2)}) async-start(), calls=%async_computation.5 | async-start | bytes 524288 | tf_op jit(solution)/shard_map/psum | solution.py:176
  144.1 1.0 copy-start.6
  171.0 0.9 copy-start
  173.6 162.8 %reduce-scatter.5.cloned.1.call-start = ((), (), s32[]{:S(2)}) async-start(), calls=%async_computation.4 | async-start | bytes 1179648 | tf_op jit(solution)/shard_map/reduce_scatter | solution.py:180
  188.1 3.4 copy-start.3
  297.8 0.9 copy-start.7
  336.4 0.9 copy-start.1
Sparse Core Ops, SparseCore 0:
  14.3 129.7 all-reduce.2
  173.7 124.0 all-reduce.4
  301.0 35.3 reduce-scatter.4
Sparse Core Ops, SparseCore 1:
  38.8 25.3 reduce-scatter.2
where the time goes:
time: 346 us
  waiting for transfers between devices  213 us (62%)
  Pallas kernels  75.1 us (22%)
  blocking collectives  26 us (8%)
  between operations  15.9 us (5%)
  local copies, waits for them, and re-layouts  13.5 us (4%)
    psum x1, waiting for transfers between devices, local(): gram_b = lax.psum(dot(factor_b, factor_b, 0, 0), ('wide', 'narrow'))  105 us
    psum x1, waiting for transfers between devices, local(): gram_a = lax.psum(gram_a, ('wide', 'narrow'))  96.1 us
    pallas_call x2, Pallas kernels, inverse_root(): pl.pallas_call(root_kernel, out_shape=jax.ShapeDtypeStruct((rank, rank),...  51.7 us
    pallas_call x2, Pallas kernels, mix_pass(): pl.pallas_call(functools.partial(pass_kernel, first, rows), out_shape=jax...  20.2 us
    all_gather x1, blocking collectives, local(): a_rows = lax.all_gather(a_half, 'narrow', axis=0, tiled=True)  14.4 us
    unnamed x28, local copies, waits for them, and re-layouts  13.5 us
    reduce_scatter x1, waiting for transfers between devices, local(): lax.psum_scatter(second_part, 'wide', scatter_dimension=0, tiled=True)  11.8 us
    all_gather x1, blocking collectives, local(): gathered = lax.all_gather(factor_b, 'wide', axis=0, tiled=True)  11.6 us
  transfers between devices with their start and end apart: 4, of which 3 were waited for; matrix products, arithmetic and copies ran while one was open for 0% of the time, Pallas kernels for 21%

commit v1 on v0

v1 whole, which is shorter than its diff:
```python
import functools

import jax
import jax.numpy as jnp
from jax import lax
from jax.experimental import pallas as pl
from jax.experimental.pallas import tpu as pltpu
from jax.sharding import PartitionSpec as P

VMEM = pl.BlockSpec(memory_space=pltpu.VMEM)
HIGH = lax.Precision.HIGHEST
NB = 64


def dot(x, y, x_dim, y_dim, precision=None):
    return lax.dot_general(
        x, y, (((x_dim,), (y_dim,)), ((), ())), precision=precision,
        preferred_element_type=jnp.float32,
    )


def pass_kernel(first, rows, load_id, store_id, depth_id, count, x_ref, c_ref, f_ref, out_ref):
    slot = pl.program_id(0)

    @pl.when(slot == 0)
    def _():
        out_ref[...] = jnp.zeros_like(out_ref)

    @pl.when(slot < count[0])
    def _():
        depth_rows = c_ref[pl.ds(pl.multiple_of(depth_id[slot] * rows, rows), rows), :]
        tile = f_ref[pl.ds(pl.multiple_of(load_id[slot] * rows, rows), rows), :].astype(jnp.float32)
        target = pl.multiple_of(store_id[slot] * rows, rows)
        step = 8
        total = None
        for a in range(0, rows, step):
            x = x_ref[0, :, a * rows : (a + step) * rows]
            mix = dot(x, depth_rows, 0, 0).reshape(step, rows, -1)
            if first:
                at = pl.ds(target + a, step)
                out_ref[at, :] += jnp.sum(mix * tile[None], axis=1)
            else:
                term = jnp.sum(mix * tile[a : a + step][:, None, :], axis=0)
                total = term if total is None else total + term
        if not first:
            out_ref[pl.ds(target, rows), :] += total


def mix_pass(first, x, load_id, store_id, depth_id, count, c, f, out_rows):
    cap, rows, width = x.shape
    rank = c.shape[1]
    whole = lambda a: pl.BlockSpec(a.shape, lambda s, *_: (0, 0))
    return pl.pallas_call(
        functools.partial(pass_kernel, first, rows),
        out_shape=jax.ShapeDtypeStruct((out_rows, rank), jnp.float32),
        grid_spec=pltpu.PrefetchScalarGridSpec(
            num_scalar_prefetch=4,
            grid=(cap,),
            in_specs=[
                pl.BlockSpec(
                    (1, rows, width),
                    lambda s, l, t, d, n: (jnp.minimum(s, n[0] - 1), 0, 0),
                ),
                whole(c),
                whole(f),
            ],
            out_specs=pl.BlockSpec((out_rows, rank), lambda s, *_: (0, 0)),
        ),
        cost_estimate=pl.CostEstimate(
            flops=cap * rows * width * rank * 8, bytes_accessed=x.size * 2, transcendentals=0
        ),
        compiler_params=pltpu.CompilerParams(vmem_limit_bytes=40 * 1024 * 1024),
    )(load_id, store_id, depth_id, count, x, c, f)


def root_steps(gram_ref, gram_c_ref, w_ref, work):
    rank = gram_ref.shape[0]
    pair = 2 * NB
    work[:, :rank] = gram_ref[...] * gram_c_ref[...]
    row_id = lax.broadcasted_iota(jnp.int32, (rank, rank), 0)
    col_id = lax.broadcasted_iota(jnp.int32, (rank, rank), 1)
    work[:, rank:] = (row_id == col_id).astype(jnp.float32)
    row = lax.broadcasted_iota(jnp.int32, (NB, pair), 0)
    lane = lax.broadcasted_iota(jnp.int32, (NB, pair), 1)
    sub = row[:8]

    for k in range(rank // NB):
        lo, hi = k * NB, (k + 1) * NB
        at = lo // pair * pair
        tile = work[lo:hi, at : at + pair]
        if lo != at:
            tile = pltpu.roll(tile, NB, 1)
        full = jnp.where(lane < NB, tile, (lane - NB == row).astype(jnp.float32))
        parts = [full[i : i + 8] for i in range(0, NB, 8)]
        for j in range(0, NB, 2):
            top, inner = j // 8, j % 8
            rest = range(top, NB // 8)
            first = {i: jnp.broadcast_to(parts[i][:, j : j + 1], (8, pair)) for i in rest}
            second = {i: jnp.broadcast_to(parts[i][:, j + 1 : j + 2], (8, pair)) for i in rest}
            row0 = parts[top][inner : inner + 1, :]
            row1 = parts[top][inner + 1 : inner + 2, :]
            p = first[top][inner : inner + 1, :]
            q = second[top][inner : inner + 1, :]
            r = second[top][inner + 1 : inner + 2, :]
            inverse = 1.0 / (p * r - q * q)
            scaled0 = (r * row0 - q * row1) * inverse
            scaled1 = (p * row1 - q * row0) * inverse
            for i in rest:
                if i == top and inner == 6:
                    continue
                term = first[i] * scaled0 + second[i] * scaled1
                if i == top:
                    term = jnp.where(sub > inner + 1, term, 0.0)
                parts[i] = parts[i] - term
        done = jnp.concatenate(parts, axis=0)
        above = pltpu.roll(done, 1, 0)
        odd = row % 2 == 1
        before = lane == row - 1
        p = jnp.sum(jnp.where(before, above, 0.0), axis=1, keepdims=True)
        q = jnp.sum(jnp.where(before, done, 0.0), axis=1, keepdims=True)
        ratio = q / jnp.where(odd, p, 1.0)
        done = jnp.where(odd, done - ratio * above, done)
        diag = jnp.sum(jnp.where(lane == row, done, 0.0), axis=1, keepdims=True)
        root = (done * lax.rsqrt(diag))[:, NB:]
        stop = rank + (hi + pair - 1) // pair * pair
        w_ref[lo:hi, :] = jnp.zeros((NB, rank), jnp.float32)
        tail = dot(root, work[lo:hi, rank:stop], 1, 0, HIGH)
        w_ref[lo:hi, : stop - rank] = tail
        if hi < rank:
            start = hi // pair * pair
            head = dot(root, work[lo:hi, start:rank], 1, 0, HIGH)
            work[start:rank, start:rank] -= dot(head, head, 0, 0, HIGH)
            work[hi:rank, rank:stop] -= dot(head, tail, 0, 0, HIGH)[hi - start :]


def inverse_root(gram, gram_c):
    rank = gram.shape[0]
    return pl.pallas_call(
        root_steps,
        out_shape=jax.ShapeDtypeStruct((rank, rank), jnp.float32),
        in_specs=[VMEM] * 2,
        out_specs=VMEM,
        scratch_shapes=[pltpu.VMEM((rank, 2 * rank), jnp.float32)],
        compiler_params=pltpu.CompilerParams(vmem_limit_bytes=40 * 1024 * 1024),
    )(gram, gram_c)


def greet(axes):
    barrier = pltpu.get_barrier_semaphore()
    total = 0
    for axis, n in axes.items():
        me = lax.axis_index(axis)
        for k in range(1, n):
            pl.semaphore_signal(
                barrier, inc=1, device_id={axis: lax.rem(me + k, n)}, device_id_type=pl.DeviceIdType.MESH
            )
        total += n - 1
    pl.semaphore_wait(barrier, total)


def exchange(axis, n, source, target, sems):
    me = lax.axis_index(axis)
    copies = []
    for k in range(1, n):
        peer = lax.rem(me + k, n)
        copy = pltpu.make_async_remote_copy(
            src_ref=source(peer),
            dst_ref=target,
            send_sem=sems.at[0, k - 1],
            recv_sem=sems.at[1, k - 1],
            device_id={axis: peer},
            device_id_type=pl.DeviceIdType.MESH,
        )
        copy.start()
        copies.append(copy)
    return copies


def finish(copies):
    for copy in copies:
        copy.wait()


def added(stage, n):
    total = stage[0]
    for i in range(1, n):
        total = total + stage[i]
    return total


def share(index, rows):
    return pl.ds(pl.multiple_of(index * rows, rows), rows)


def sum_all(wide, narrow, part, out, stage_w, stage_n, sems_w, sems_n, sems_g, beside=None):
    me_w, me_n = lax.axis_index("wide"), lax.axis_index("narrow")
    rows = part.shape[0] // wide
    mine = share(me_w, rows)
    copies = exchange("wide", wide, lambda peer: part.at[share(peer, rows)], stage_w.at[me_w], sems_w)
    stage_w[me_w] = part[mine, :]
    if beside is not None:
        beside()
    finish(copies)
    stage_n[me_n] = added(stage_w, wide)
    finish(exchange("narrow", narrow, lambda peer: stage_n.at[me_n], stage_n.at[me_n], sems_n))
    out[mine, :] = added(stage_n, narrow)
    finish(exchange("wide", wide, lambda peer: out.at[mine], out.at[mine], sems_g))


def sum_scratch(wide, narrow, rank):
    return [
        pltpu.VMEM((rank, rank), jnp.float32),
        pltpu.VMEM((wide, rank // wide, rank), jnp.float32),
        pltpu.VMEM((narrow, rank // wide, rank), jnp.float32),
        pltpu.SemaphoreType.DMA((2, wide)),
        pltpu.SemaphoreType.DMA((2, narrow)),
        pltpu.SemaphoreType.DMA((2, wide)),
    ]


def params(collective):
    return pltpu.CompilerParams(
        collective_id=collective, has_side_effects=True, vmem_limit_bytes=40 * 1024 * 1024
    )


def start_kernel(wide, narrow, b_ref, c_ref, rows_ref, gram_ref, gram_c_ref, part, *rest):
    *sum_rest, sems = rest
    me = lax.axis_index("wide")
    rows = b_ref.shape[0]
    greet({"wide": wide, "narrow": narrow})
    b = b_ref[...]
    part[...] = dot(b, b, 0, 0)
    mine = share(me, rows)

    def beside():
        rows_ref[mine, :] = b
        c = c_ref[...]
        gram_c_ref[...] = dot(c, c, 0, 0)

    copies = exchange("wide", wide, lambda peer: b_ref, rows_ref.at[mine], sems)
    sum_all(wide, narrow, part, gram_ref, *sum_rest, beside)
    finish(copies)


def start(wide, narrow, b, c):
    rows, rank = b.shape
    return pl.pallas_call(
        functools.partial(start_kernel, wide, narrow),
        out_shape=[
            jax.ShapeDtypeStruct((wide * rows, rank), b.dtype),
            jax.ShapeDtypeStruct((rank, rank), jnp.float32),
            jax.ShapeDtypeStruct((rank, rank), jnp.float32),
        ],
        in_specs=[VMEM] * 2,
        out_specs=[VMEM] * 3,
        scratch_shapes=sum_scratch(wide, narrow, rank) + [pltpu.SemaphoreType.DMA((2, wide))],
        compiler_params=params(0),
    )(b, c)


def middle_kernel(wide, narrow, sum_ref, w_ref, new_ref, rows_ref, gram_ref, part, *rest):
    *sum_rest, stage, sems, sems_a = rest
    me = lax.axis_index("narrow")
    rows = new_ref.shape[0]
    greet({"wide": wide, "narrow": narrow})
    mine = share(me, rows)
    copies = exchange("narrow", narrow, lambda peer: sum_ref.at[share(peer, rows)], stage.at[me], sems)
    stage[me] = sum_ref[mine, :]
    finish(copies)
    w = w_ref[...]
    new = dot(dot(added(stage, narrow), w, 1, 1, HIGH), w, 1, 0, HIGH)
    half = new.astype(jnp.bfloat16)
    rows_ref[mine, :] = half
    copies = exchange("narrow", narrow, lambda peer: rows_ref.at[mine], rows_ref.at[mine], sems_a)
    part[...] = dot(half, half, 0, 0)

    def beside():
        new_ref[...] = new

    sum_all(wide, narrow, part, gram_ref, *sum_rest, beside)
    finish(copies)


def middle(wide, narrow, first_part, w):
    rows, rank = first_part.shape[0] // narrow, first_part.shape[1]
    return pl.pallas_call(
        functools.partial(middle_kernel, wide, narrow),
        out_shape=[
            jax.ShapeDtypeStruct((rows, rank), jnp.float32),
            jax.ShapeDtypeStruct((narrow * rows, rank), jnp.bfloat16),
            jax.ShapeDtypeStruct((rank, rank), jnp.float32),
        ],
        in_specs=[VMEM] * 2,
        out_specs=[VMEM] * 3,
        scratch_shapes=sum_scratch(wide, narrow, rank)
        + [
            pltpu.VMEM((narrow, rows, rank), jnp.float32),
            pltpu.SemaphoreType.DMA((2, narrow)),
            pltpu.SemaphoreType.DMA((2, narrow)),
        ],
        compiler_params=params(1),
    )(first_part, w)


def last_kernel(wide, sum_ref, w_ref, new_ref, stage, sems):
    me = lax.axis_index("wide")
    rows = new_ref.shape[0]
    greet({"wide": wide})
    copies = exchange("wide", wide, lambda peer: sum_ref.at[share(peer, rows)], stage.at[me], sems)
    stage[me] = sum_ref[share(me, rows), :]
    finish(copies)
    w = w_ref[...]
    new_ref[...] = dot(dot(added(stage, wide), w, 1, 1, HIGH), w, 1, 0, HIGH)


def last(wide, second_part, w):
    rows, rank = second_part.shape[0] // wide, second_part.shape[1]
    return pl.pallas_call(
        functools.partial(last_kernel, wide),
        out_shape=jax.ShapeDtypeStruct((rows, rank), jnp.float32),
        in_specs=[VMEM] * 2,
        out_specs=VMEM,
        scratch_shapes=[
            pltpu.VMEM((wide, rows, rank), jnp.float32),
            pltpu.SemaphoreType.DMA((2, wide)),
        ],
        compiler_params=params(2),
    )(second_part, w)


def local(blocks, row_tile, col_tile, depth_tile, block_count, factor_b, factor_c):
    x = blocks[0, 0]
    first_ids = row_tile[0, 0]
    second_ids = col_tile[0, 0]
    depth_ids = depth_tile[0, 0]
    count = block_count[0]
    wide = lax.axis_size("wide")
    narrow = lax.axis_size("narrow")
    rows = factor_b.shape[0]

    b_rows, gram_b, gram_c = start(wide, narrow, factor_b, factor_c)
    first_part = mix_pass(
        True, x, second_ids, first_ids, depth_ids, count, factor_c, b_rows, narrow * rows
    )
    a_new, a_rows, gram_a = middle(wide, narrow, first_part, inverse_root(gram_b, gram_c))
    second_part = mix_pass(
        False, x, first_ids, second_ids, depth_ids, count, factor_c, a_rows, wide * rows
    )
    b_new = last(wide, second_part, inverse_root(gram_a, gram_c))
    return (a_new, b_new)


def solution(mesh):
    return jax.shard_map(
        local,
        mesh=mesh,
        in_specs=(
            P("wide", "narrow", None, None, None),
            P("wide", "narrow", None),
            P("wide", "narrow", None),
            P("wide", "narrow", None),
            P("wide", "narrow"),
            P(("wide", "narrow"), None),
            P(),
        ),
        out_specs=(P(("wide", "narrow"), None), P(("wide", "narrow"), None)),
        check_vma=False,
    )
```

time: 346 us -> 134 us (0.39)
  waiting for transfers between devices: 213 us -> 0 us
  Pallas kernels: 75.1 us -> 121 us
  blocking collectives: 26 us -> 0 us
  between operations: 15.9 us -> 1.38 us
  local copies, waits for them, and re-layouts: 13.5 us -> 9.58 us
    psum x2 -> x0, waiting for transfers between devices: 202 us -> none  [the longest x1 105 us: local(): gram_b = lax.psum(dot(factor_b, factor_b, 0, 0), ('wide', 'narrow'))]
    pallas_call x4 -> x5, Pallas kernels: 54.8 us -> 111 us  [the longest x1 37.5 us: middle(): pl.pallas_call(functools.partial(middle_kernel, wide, narrow), out_shape=...]
    all_gather x2 -> x0, blocking collectives: 26 us -> none  [the longest x1 14.4 us: local(): a_rows = lax.all_gather(a_half, 'narrow', axis=0, tiled=True)]
    reduce_scatter x2 -> x0, waiting for transfers between devices: 11.8 us -> none  [the longest x1 11.8 us: local(): lax.psum_scatter(second_part, 'wide', scatter_dimension=0, tiled=True)]
    pallas_call x2, Pallas kernels: 20.2 us -> 9.47 us  [mix_pass(): pl.pallas_call(functools.partial(pass_kernel, first, rows), out_shape=jax...]
    unnamed x28 -> x22, local copies, waits for them, and re-layouts: 13.5 us -> 9.58 us
  transfers between devices with their start and end apart: 4 -> 0, of which waited for: 3 -> 0; matrix products, arithmetic and copies ran while one was open for 0% -> 0% of each run, Pallas kernels for 21% -> 0%
where the time goes in v1:
time: 134 us; the launch traced here: 132 us
  Pallas kernels  121 us (90%)
  local copies, waits for them, and re-layouts  9.58 us (7%)
  between operations  1.38 us (1%)
    pallas_call x1, Pallas kernels, middle(): pl.pallas_call(functools.partial(middle_kernel, wide, narrow), out_shape=...  37.5 us
    pallas_call x2, Pallas kernels, inverse_root(): pl.pallas_call(root_steps, out_shape=jax.ShapeDtypeStruct((rank, rank), j...  29.1 us
    pallas_call x1, Pallas kernels, start(): pl.pallas_call(functools.partial(start_kernel, wide, narrow), out_shape=[...  24.4 us
    pallas_call x1, Pallas kernels, last(): pl.pallas_call(functools.partial(last_kernel, wide), out_shape=jax.ShapeD...  20.3 us
    unnamed x22, local copies, waits for them, and re-layouts  9.58 us
    pallas_call x2, Pallas kernels, mix_pass(): pl.pallas_call(functools.partial(pass_kernel, first, rows), out_shape=jax...  9.47 us

profile of v1, /device:TPU:0, one launch (start us, length us, event | category | flops | bytes accessed | tf_op | source)
XLA Modules:
  0.0 131.9 jit_solution(9265125463281160665)
XLA Ops:
  1.3 0.0 copy-start
  1.3 1.0 copy-done
  2.3 0.0 copy-start.3
  2.3 0.8 copy-done.3
  3.2 24.4 %shard_map.86 = (bf16[1024,256]{1,0:T(8,128)(2,1)S(1)}, f32[256,256]{1,0:T(8,128)S(1)}, f32[256,256]{1,0:T(8,128)S(1)}) custom-call(bf16[128,256]{1,0:T(8,128)(2,1)S(1)} %copy-done.3, bf16[1024,256]{1,0:T(8,128)(2,1)S(1)} %copy-done), custom_call_target="tpu_custom_call" | custom-call | tf_op jit(solution)/shard_map/pallas_call | solution.py:248
  27.6 0.0 copy-start.1
  27.6 1.0 copy-done.1
  28.6 0.0 copy-start.4
  28.6 3.4 %copy-done.4 = bf16[1,1,16,64,4096]{4,3,2,1,0:T(8,128)(2,1)S(1)} copy-done((bf16[1,1,16,64,4096]{4,3,2,1,0:T(8,128)(2,1)S(1)}, bf16[1,1,16,64,4096]{4,3,2,1,0:T(8,128)(2,1)}, u32[]{:S(2)}) %copy-start.4) | copy-done | bytes 8388632
  32.0 0.0 copy-start.6
  32.0 0.7 copy-done.6
  32.7 0.7 copy-done.8
  33.3 0.7 copy-done.9
  34.0 4.7 %shard_map.87.sum_ref = f32[512,256]{1,0:T(8,128)S(1)} custom-call(s32[16]{0:T(128)S(1)} %bitcast.9, s32[16]{0:T(128)S(1)} %bitcast.11, s32[16]{0:T(128)S(1)} %bitcast.13, s32[1]{0:T(128)} %bitcast.5.count, bf16[16,64,4096]{2,1,0:T(8,128)(2,1)S(1)} %bitcast.7, bf16[1024,256]{1,0:T(8,128)(2,1)S(1)} %copy-done.1, bf16[1024,256]{1,0:T(8,128)(2,1)S(1)} %get-tuple-element.8.f_ref), custom_call_target="tpu_custom_call" | custom-call | flops 8589934592 | bytes 8388608 | tf_op jit(solution)/shard_map/pallas_call | solution.py:53
  38.7 14.6 %shard_map.88.w_ref = f32[256,256]{1,0:T(8,128)S(1)} custom-call(f32[256,256]{1,0:T(8,128)S(1)} %get-tuple-element.9.gram_ref, f32[256,256]{1,0:T(8,128)S(1)} %get-tuple-element.10.gram_c_ref), custom_call_target="tpu_custom_call" | custom-call | tf_op jit(solution)/shard_map/pallas_call | solution.py:138
  53.3 37.5 %shard_map.89 = (f32[128,256]{1,0:T(8,128)S(1)}, bf16[512,256]{1,0:T(8,128)(2,1)S(1)}, f32[256,256]{1,0:T(8,128)S(1)}) custom-call(f32[512,256]{1,0:T(8,128)S(1)} %shard_map.87.sum_ref, f32[256,256]{1,0:T(8,128)S(1)} %shard_map.88.w_ref), custom_call_target="tpu_custom_call" | custom-call | tf_op jit(solution)/shard_map/pallas_call | solution.py:287
  90.9 14.6 %shard_map.91.w_ref = f32[256,256]{1,0:T(8,128)S(1)} custom-call(f32[256,256]{1,0:T(8,128)S(1)} %get-tuple-element.13.gram_ref, f32[256,256]{1,0:T(8,128)S(1)} %get-tuple-element.10.gram_c_ref), custom_call_target="tpu_custom_call" | custom-call | tf_op jit(solution)/shard_map/pallas_call | solution.py:138
  105.4 0.0 copy-done.2
  105.5 0.0 copy-done.5
  105.5 0.0 copy-done.7
  105.5 4.7 %shard_map.90.sum_ref = f32[1024,256]{1,0:T(8,128)S(1)} custom-call(s32[16]{0:T(128)S(1)} %bitcast.12, s32[16]{0:T(128)S(1)} %bitcast.10, s32[16]{0:T(128)S(1)} %bitcast.14, s32[1]{0:T(128)} %bitcast.6.count, bf16[16,64,4096]{2,1,0:T(8,128)(2,1)S(1)} %bitcast.8, bf16[1024,256]{1,0:T(8,128)(2,1)S(1)} %copy-done.2, bf16[512,256]{1,0:T(8,128)(2,1)S(1)} %get-tuple-element.12.f_ref), custom_call_target="tpu_custom_call" | custom-call | flops 8589934592 | bytes 8388608 | tf_op jit(solution)/shard_map/pallas_call | solution.py:53
  110.2 20.3 %shard_map.92 = f32[128,256]{1,0:T(8,128)S(1)} custom-call(f32[1024,256]{1,0:T(8,128)S(1)} %shard_map.90.sum_ref, f32[256,256]{1,0:T(8,128)S(1)} %shard_map.91.w_ref), custom_call_target="tpu_custom_call" | custom-call | tf_op jit(solution)/shard_map/pallas_call | solution.py:319
  130.5 0.7 copy.12
  131.2 0.7 copy.13
  (5 shorter events, 0.0 us)
Async XLA Ops:
  1.3 1.0 copy-start
  2.3 0.8 copy-start.3
  27.6 1.0 copy-start.1
  28.6 3.4 %copy-start.4 = (bf16[1,1,16,64,4096]{4,3,2,1,0:T(8,128)(2,1)S(1)}, bf16[1,1,16,64,4096]{4,3,2,1,0:T(8,128)(2,1)}, u32[]{:S(2)}) copy-start(bf16[1,1,16,64,4096]{4,3,2,1,0:T(8,128)(2,1)} %param.7) | copy-start | bytes 25165828
  32.0 0.7 copy-start.6
  32.7 0.7 copy-start.8
  33.3 0.7 copy-start.9
  34.0 71.5 %copy-start.2 = (bf16[1024,256]{1,0:T(8,128)(2,1)S(1)}, bf16[1024,256]{1,0:T(8,128)(2,1)}, u32[]{:S(2)}) copy-start(bf16[1024,256]{1,0:T(8,128)(2,1)} %c_ref.5) | copy-start | bytes 1572868
  34.0 71.5 %copy-start.5 = (bf16[1,1,16,64,4096]{4,3,2,1,0:T(8,128)(2,1)S(1)}, bf16[1,1,16,64,4096]{4,3,2,1,0:T(8,128)(2,1)}, u32[]{:S(2)}) copy-start(bf16[1,1,16,64,4096]{4,3,2,1,0:T(8,128)(2,1)} %param.7) | copy-start | bytes 25165828
  34.0 71.5 %copy-start.7 = (s32[1,1,16]{2,1,0:T(1,128)S(1)}, s32[1,1,16]{2,1,0:T(1,128)}, u32[]{:S(2)}) copy-start(s32[1,1,16]{2,1,0:T(1,128)} %param.9) | copy-start | bytes 196

commit v2 on v1

--- a/solution.py
+++ b/solution.py
@@ -82,7 +82,6 @@
     work[:, rank:] = (row_id == col_id).astype(jnp.float32)
     row = lax.broadcasted_iota(jnp.int32, (NB, pair), 0)
     lane = lax.broadcasted_iota(jnp.int32, (NB, pair), 1)
-    sub = row[:8]
 
     for k in range(rank // NB):
         lo, hi = k * NB, (k + 1) * NB
@@ -91,27 +90,25 @@
         if lo != at:
             tile = pltpu.roll(tile, NB, 1)
         full = jnp.where(lane < NB, tile, (lane - NB == row).astype(jnp.float32))
-        parts = [full[i : i + 8] for i in range(0, NB, 8)]
+        parts = []
         for j in range(0, NB, 2):
-            top, inner = j // 8, j % 8
-            rest = range(top, NB // 8)
-            first = {i: jnp.broadcast_to(parts[i][:, j : j + 1], (8, pair)) for i in rest}
-            second = {i: jnp.broadcast_to(parts[i][:, j + 1 : j + 2], (8, pair)) for i in rest}
-            row0 = parts[top][inner : inner + 1, :]
-            row1 = parts[top][inner + 1 : inner + 2, :]
-            p = first[top][inner : inner + 1, :]
-            q = second[top][inner : inner + 1, :]
-            r = second[top][inner + 1 : inner + 2, :]
+            inner = j % 8
+            if inner == 0 and j > 0:
+                parts.append(full[:8])
+                full = full[8:]
+            first = jnp.broadcast_to(full[:, j : j + 1], full.shape)
+            second = jnp.broadcast_to(full[:, j + 1 : j + 2], full.shape)
+            row0 = full[inner : inner + 1, :]
+            row1 = full[inner + 1 : inner + 2, :]
+            p = first[inner : inner + 1, :]
+            q = second[inner : inner + 1, :]
+            r = second[inner + 1 : inner + 2, :]
             inverse = 1.0 / (p * r - q * q)
             scaled0 = (r * row0 - q * row1) * inverse
             scaled1 = (p * row1 - q * row0) * inverse
-            for i in rest:
-                if i == top and inner == 6:
-                    continue
-                term = first[i] * scaled0 + second[i] * scaled1
-                if i == top:
-                    term = jnp.where(sub > inner + 1, term, 0.0)
-                parts[i] = parts[i] - term
+            term = first * scaled0 + second * scaled1
+            full = full - jnp.where(row[: full.shape[0]] > inner + 1, term, 0.0)
+        parts.append(full)
         done = jnp.concatenate(parts, axis=0)
         above = pltpu.roll(done, 1, 0)
         odd = row % 2 == 1
@@ -133,18 +130,6 @@
             work[hi:rank, rank:stop] -= dot(head, tail, 0, 0, HIGH)[hi - start :]
 
 
-def inverse_root(gram, gram_c):
-    rank = gram.shape[0]
-    return pl.pallas_call(
-        root_steps,
-        out_shape=jax.ShapeDtypeStruct((rank, rank), jnp.float32),
-        in_specs=[VMEM] * 2,
-        out_specs=VMEM,
-        scratch_shapes=[pltpu.VMEM((rank, 2 * rank), jnp.float32)],
-        compiler_params=pltpu.CompilerParams(vmem_limit_bytes=40 * 1024 * 1024),
-    )(gram, gram_c)
-
-
 def greet(axes):
     barrier = pltpu.get_barrier_semaphore()
     total = 0
@@ -259,14 +244,15 @@
     )(b, c)
 
 
-def middle_kernel(wide, narrow, sum_ref, w_ref, new_ref, rows_ref, gram_ref, part, *rest):
-    *sum_rest, stage, sems, sems_a = rest
+def middle_kernel(wide, narrow, sum_ref, gram_b_ref, gram_c_ref, new_ref, rows_ref, gram_ref, part, *rest):
+    *sum_rest, stage, sems, sems_a, w_ref, work = rest
     me = lax.axis_index("narrow")
     rows = new_ref.shape[0]
     greet({"wide": wide, "narrow": narrow})
     mine = share(me, rows)
     copies = exchange("narrow", narrow, lambda peer: sum_ref.at[share(peer, rows)], stage.at[me], sems)
     stage[me] = sum_ref[mine, :]
+    root_steps(gram_b_ref, gram_c_ref, w_ref, work)
     finish(copies)
     w = w_ref[...]
     new = dot(dot(added(stage, narrow), w, 1, 1, HIGH), w, 1, 0, HIGH)
@@ -282,7 +268,7 @@
     finish(copies)
 
 
-def middle(wide, narrow, first_part, w):
+def middle(wide, narrow, first_part, gram_b, gram_c):
     rows, rank = first_part.shape[0] // narrow, first_part.shape[1]
     return pl.pallas_call(
         functools.partial(middle_kernel, wide, narrow),
@@ -291,42 +277,47 @@
             jax.ShapeDtypeStruct((narrow * rows, rank), jnp.bfloat16),
             jax.ShapeDtypeStruct((rank, rank), jnp.float32),
         ],
-        in_specs=[VMEM] * 2,
+        in_specs=[VMEM] * 3,
         out_specs=[VMEM] * 3,
         scratch_shapes=sum_scratch(wide, narrow, rank)
         + [
             pltpu.VMEM((narrow, rows, rank), jnp.float32),
             pltpu.SemaphoreType.DMA((2, narrow)),
             pltpu.SemaphoreType.DMA((2, narrow)),
+            pltpu.VMEM((rank, rank), jnp.float32),
+            pltpu.VMEM((rank, 2 * rank), jnp.float32),
         ],
         compiler_params=params(1),
-    )(first_part, w)
-
-
-def last_kernel(wide, sum_ref, w_ref, new_ref, stage, sems):
+    )(first_part, gram_b, gram_c)
+
+
+def last_kernel(wide, sum_ref, gram_a_ref, gram_c_ref, new_ref, stage, sems, w_ref, work):
     me = lax.axis_index("wide")
     rows = new_ref.shape[0]
     greet({"wide": wide})
     copies = exchange("wide", wide, lambda peer: sum_ref.at[share(peer, rows)], stage.at[me], sems)
     stage[me] = sum_ref[share(me, rows), :]
+    root_steps(gram_a_ref, gram_c_ref, w_ref, work)
     finish(copies)
     w = w_ref[...]
     new_ref[...] = dot(dot(added(stage, wide), w, 1, 1, HIGH), w, 1, 0, HIGH)
 
 
-def last(wide, second_part, w):
+def last(wide, second_part, gram_a, gram_c):
     rows, rank = second_part.shape[0] // wide, second_part.shape[1]
     return pl.pallas_call(
         functools.partial(last_kernel, wide),
         out_shape=jax.ShapeDtypeStruct((rows, rank), jnp.float32),
-        in_specs=[VMEM] * 2,
+        in_specs=[VMEM] * 3,
         out_specs=VMEM,
         scratch_shapes=[
             pltpu.VMEM((wide, rows, rank), jnp.float32),
             pltpu.SemaphoreType.DMA((2, wide)),
+            pltpu.VMEM((rank, rank), jnp.float32),
+            pltpu.VMEM((rank, 2 * rank), jnp.float32),
         ],
         compiler_params=params(2),
-    )(second_part, w)
+    )(second_part, gram_a, gram_c)
 
 
 def local(blocks, row_tile, col_tile, depth_tile, block_count, factor_b, factor_c):
@@ -343,11 +334,11 @@
     first_part = mix_pass(
         True, x, second_ids, first_ids, depth_ids, count, factor_c, b_rows, narrow * rows
     )
-    a_new, a_rows, gram_a = middle(wide, narrow, first_part, inverse_root(gram_b, gram_c))
+    a_new, a_rows, gram_a = middle(wide, narrow, first_part, gram_b, gram_c)
     second_part = mix_pass(
         False, x, first_ids, second_ids, depth_ids, count, factor_c, a_rows, wide * rows
     )
-    b_new = last(wide, second_part, inverse_root(gram_a, gram_c))
+    b_new = last(wide, second_part, gram_a, gram_c)
     return (a_new, b_new)
 
 

time: 134 us -> 108 us (0.81); the launches traced: 132 us -> 108 us
  Pallas kernels: 121 us -> 97.5 us
    pallas_call x2 -> x0, Pallas kernels: 29.1 us -> none  [inverse_root(): pl.pallas_call(root_steps, out_shape=jax.ShapeDtypeStruct((rank, rank), j...]
    pallas_call x2, Pallas kernels: 9.47 us -> 13.9 us  [mix_pass(): pl.pallas_call(functools.partial(pass_kernel, first, rows), out_shape=jax...]
    pallas_call x1, Pallas kernels: 20.3 us -> 21.9 us  [last(): pl.pallas_call(functools.partial(last_kernel, wide), out_shape=jax.ShapeD...]
    unnamed x22 -> x20, local copies, waits for them, and re-layouts: 9.58 us -> 9.58 us
where the time goes in v2:
time: 108 us
  Pallas kernels  97.5 us (90%)
  local copies, waits for them, and re-layouts  9.58 us (9%)
  between operations  1.36 us (1%)
    pallas_call x1, Pallas kernels, middle(): pl.pallas_call(functools.partial(middle_kernel, wide, narrow), out_shape=...  37.2 us
    pallas_call x1, Pallas kernels, start(): pl.pallas_call(functools.partial(start_kernel, wide, narrow), out_shape=[...  24.4 us
    pallas_call x1, Pallas kernels, last(): pl.pallas_call(functools.partial(last_kernel, wide), out_shape=jax.ShapeD...  21.9 us
    pallas_call x2, Pallas kernels, mix_pass(): pl.pallas_call(functools.partial(pass_kernel, first, rows), out_shape=jax...  13.9 us
    unnamed x20, local copies, waits for them, and re-layouts  9.58 us

profile of v2, /device:TPU:0, one launch (start us, length us, event | category | flops | bytes accessed | tf_op | source)
XLA Modules:
  0.0 108.4 jit_solution(8004799412182451517)
XLA Ops:
  1.3 0.0 copy-start
  1.3 1.0 copy-done
  2.3 0.0 copy-start.3
  2.3 0.8 copy-done.3
  3.2 24.4 %shard_map.86 = (bf16[1024,256]{1,0:T(8,128)(2,1)S(1)}, f32[256,256]{1,0:T(8,128)S(1)}, f32[256,256]{1,0:T(8,128)S(1)}) custom-call(bf16[128,256]{1,0:T(8,128)(2,1)S(1)} %copy-done.3, bf16[1024,256]{1,0:T(8,128)(2,1)S(1)} %copy-done), custom_call_target="tpu_custom_call" | custom-call | tf_op jit(solution)/shard_map/pallas_call | solution.py:233
  27.6 0.0 copy-start.1
  27.6 1.0 copy-done.1
  28.6 0.0 copy-start.4
  28.6 3.4 %copy-done.4 = bf16[1,1,16,64,4096]{4,3,2,1,0:T(8,128)(2,1)S(1)} copy-done((bf16[1,1,16,64,4096]{4,3,2,1,0:T(8,128)(2,1)S(1)}, bf16[1,1,16,64,4096]{4,3,2,1,0:T(8,128)(2,1)}, u32[]{:S(2)}) %copy-start.4) | copy-done | bytes 8388632
  32.0 0.0 copy-start.6
  32.0 0.7 copy-done.6
  32.7 0.0 copy-start.7
  32.7 0.7 copy-done.7
  33.3 0.0 copy-start.8
  33.3 0.7 copy-done.8
  34.0 0.0 copy-start.2
  34.0 7.0 %shard_map.87.sum_ref = f32[512,256]{1,0:T(8,128)S(1)} custom-call(s32[16]{0:T(128)S(1)} %bitcast.9, s32[16]{0:T(128)S(1)} %bitcast.11, s32[16]{0:T(128)S(1)} %bitcast.13, s32[1]{0:T(128)} %bitcast.5.count, bf16[16,64,4096]{2,1,0:T(8,128)(2,1)S(1)} %bitcast.7, bf16[1024,256]{1,0:T(8,128)(2,1)S(1)} %copy-done.1, bf16[1024,256]{1,0:T(8,128)(2,1)S(1)} %get-tuple-element.8.f_ref), custom_call_target="tpu_custom_call" | custom-call | flops 8589934592 | bytes 8388608 | tf_op jit(solution)/shard_map/pallas_call | solution.py:53
  41.0 37.2 %shard_map.88 = (f32[128,256]{1,0:T(8,128)S(1)}, bf16[512,256]{1,0:T(8,128)(2,1)S(1)}, f32[256,256]{1,0:T(8,128)S(1)}) custom-call(f32[512,256]{1,0:T(8,128)S(1)} %shard_map.87.sum_ref, f32[256,256]{1,0:T(8,128)S(1)} %get-tuple-element.9.gram_b_ref, f32[256,256]{1,0:T(8,128)S(1)} %get-tuple-element.10.gram_c_ref), custom_call_target="tpu_custom_call" | custom-call | tf_op jit(solution)/shard_map/pallas_call | solution.py:273
  78.2 0.0 copy-done.2
  78.2 0.0 copy-done.5
  78.2 7.0 %shard_map.89.sum_ref = f32[1024,256]{1,0:T(8,128)S(1)} custom-call(s32[16]{0:T(128)S(1)} %bitcast.12, s32[16]{0:T(128)S(1)} %bitcast.10, s32[16]{0:T(128)S(1)} %bitcast.14, s32[1]{0:T(128)} %bitcast.6.count, bf16[16,64,4096]{2,1,0:T(8,128)(2,1)S(1)} %bitcast.8, bf16[1024,256]{1,0:T(8,128)(2,1)S(1)} %copy-done.2, bf16[512,256]{1,0:T(8,128)(2,1)S(1)} %get-tuple-element.12.f_ref), custom_call_target="tpu_custom_call" | custom-call | flops 8589934592 | bytes 8388608 | tf_op jit(solution)/shard_map/pallas_call | solution.py:53
  85.2 21.9 %shard_map.90 = f32[128,256]{1,0:T(8,128)S(1)} custom-call(f32[1024,256]{1,0:T(8,128)S(1)} %shard_map.89.sum_ref, f32[256,256]{1,0:T(8,128)S(1)} %get-tuple-element.13.gram_a_ref, f32[256,256]{1,0:T(8,128)S(1)} %get-tuple-element.10.gram_c_ref), custom_call_target="tpu_custom_call" | custom-call | tf_op jit(solution)/shard_map/pallas_call | solution.py:308
  107.1 0.7 copy.12
  107.8 0.7 copy.13
  (1 shorter events, 0.0 us)
Async XLA Ops:
  1.3 1.0 copy-start
  2.3 0.8 copy-start.3
  27.6 1.0 copy-start.1
  28.6 3.4 %copy-start.4 = (bf16[1,1,16,64,4096]{4,3,2,1,0:T(8,128)(2,1)S(1)}, bf16[1,1,16,64,4096]{4,3,2,1,0:T(8,128)(2,1)}, u32[]{:S(2)}) copy-start(bf16[1,1,16,64,4096]{4,3,2,1,0:T(8,128)(2,1)} %param.7) | copy-start | bytes 25165828
  32.0 0.7 copy-start.6
  32.7 0.7 copy-start.7
  33.3 0.7 copy-start.8
  34.0 44.2 %copy-start.2 = (bf16[1024,256]{1,0:T(8,128)(2,1)S(1)}, bf16[1024,256]{1,0:T(8,128)(2,1)}, u32[]{:S(2)}) copy-start(bf16[1024,256]{1,0:T(8,128)(2,1)} %c_ref.5) | copy-start | bytes 1572868
  34.0 44.2 %copy-start.5 = (bf16[1,1,16,64,4096]{4,3,2,1,0:T(8,128)(2,1)S(1)}, bf16[1,1,16,64,4096]{4,3,2,1,0:T(8,128)(2,1)}, u32[]{:S(2)}) copy-start(bf16[1,1,16,64,4096]{4,3,2,1,0:T(8,128)(2,1)} %param.7) | copy-start | bytes 25165828
